TPU v7x, 32 devices: a whole 2x2x4 slice. The times are simulated.
32 devices in a mesh: groups: 2 (over y), region: 4 (over x, core), dev: 4 (over z).
Axes of the slice: x: 2, y: 2, z: 4, core: 2. Of those that a mesh axis runs over, the one named last changes fastest.
Arguments:
- inner_blocks: bfloat16 [32, 192, 128, 128], P(('groups', 'region', 'dev')), parts along dimension 0, may hold values from -1 to 4
- inner_pattern: int32 [32, 2, 192], P(('groups', 'region', 'dev')), parts along dimension 0, may hold values from 0 to 63, as said below
- boundary_blocks: bfloat16 [32, 4, 12, 128, 128], P(('groups', 'region', 'dev')), parts along dimension 0, may hold values from -1 to 1
- boundary_pattern: int32 [32, 4, 2, 12], P(('groups', 'region', 'dev')), parts along dimension 0, may hold values from 0 to 63, as said below
- send_list: int32 [32, 4, 12], P(('groups', 'region', 'dev')), parts along dimension 0, may hold values from 0 to 63, as said below
- right_side: float32 [32, 262144], P(None, ('groups', 'region', 'dev')), parts along dimension 1, may hold values from -48 to 48
- initial: float32 [32, 262144], P(None, ('groups', 'region', 'dev')), parts along dimension 1, may hold values from -3 to 3
Outputs:
- solution: float32 [32, 262144], P(None, ('groups', 'region', 'dev')), parts along dimension 1
- residual: float32 [32, 262144], P(None, ('groups', 'region', 'dev')), parts along dimension 1
There are 2 independent parts, one for each index of `groups`. A program takes and returns all parts, laid end to end along the dimension named above; each array names one. Nothing has to cross between parts.
Inputs may be any that keep to these rules, and one draw needn't show every extreme that they name: `inner_pattern`: inner blocks of each device: entries 0 to 63 are the diagonal blocks (row = column), the rest come in pairs of mutually transposed blocks; Q is symmetric positive definite. `boundary_pattern`: within one device and direction the slots form a permutation of 0 to 11, and each boundary block is the transpose of the matching block on the neighbour. `send_list`: entries of one device and direction are distinct.
All inputs are finite; a program needn't handle non-finite values.
Results may differ from a plain program's by a relative error of at most 0.0017.
The roundings to bfloat16 on the way count: a program that leaves them out, or rounds other values in their place, can miss the bound.
Values may be sent and summed in bfloat16 or wider, within the bound.
A program may use at most 64 MiB of HBM per device.

v0:
```python
import jax
import jax.numpy as jnp
from jax import lax
from jax.sharding import PartitionSpec as P

ITERS = 2


def padded(value, sides, width):
    for axis, dim in sides:
        count, length = (lax.axis_size(axis), value.shape[dim])
        up = [(i, (i + 1) % count) for i in range(count)]
        down = [(j, i) for i, j in up]
        last = lax.slice_in_dim(value, length - width, length, axis=dim)
        first = lax.slice_in_dim(value, 0, width, axis=dim)
        before = lax.ppermute(last, axis, up)
        after = lax.ppermute(first, axis, down)
        value = jnp.concatenate([before, value, after], axis=dim)
    return value


def apply_precision(
    vector, inner_blocks, inner_pattern, boundary_blocks, boundary_pattern, send_list
):
    chains = vector.shape[0]
    block_size = inner_blocks.shape[-1]
    block_count = vector.shape[1] // block_size
    block_view = vector.reshape(chains, block_count, block_size)
    inner_rows = inner_pattern[0, 0]
    inner_cols = inner_pattern[0, 1]
    picked = block_view[:, inner_cols]
    product = jnp.einsum(
        "cnv,nwv->cnw", picked, inner_blocks[0], preferred_element_type=jnp.float32
    )
    placing = (inner_rows[:, None] == jnp.arange(block_count)[None, :]).astype(jnp.float32)
    summed = jnp.einsum("cnw,nb->cbw", product, placing, precision=lax.Precision.HIGHEST)
    dev_packets = block_view[:, send_list[0, 0:2]]
    dev_rim = padded(dev_packets, (("dev", 1),), 1)
    from_left = dev_rim[:, 0]
    from_right = dev_rim[:, 3]
    region_packets = block_view[:, send_list[0, 2:4]]
    region_rim = padded(region_packets, (("region", 1),), 1)
    received = [from_left, from_right, region_rim[:, 0], region_rim[:, 3]]
    slot_index = boundary_pattern[0, :, 1]
    distant = jnp.stack([received[heading][:, slot_index[heading]] for heading in range(4)])
    far_product = jnp.einsum(
        "ucev,uewv->ucew", distant, boundary_blocks[0], preferred_element_type=jnp.float32
    )
    far_placing = (boundary_pattern[0, :, 0, :, None] == jnp.arange(block_count)).astype(
        jnp.float32
    )
    summed = summed + jnp.einsum(
        "ucew,ueb->cbw", far_product, far_placing, precision=lax.Precision.HIGHEST
    )
    return summed.reshape(chains, block_count * block_size)


def local_inner(first_vec, second_vec):
    return jnp.sum(first_vec * second_vec, axis=1)


def per_device(
    inner_blocks, inner_pattern, boundary_blocks, boundary_pattern, send_list, right_side, initial
):

    def apply_now(vector):
        return apply_precision(
            vector, inner_blocks, inner_pattern, boundary_blocks, boundary_pattern, send_list
        )

    residual = right_side - apply_now(initial.astype(jnp.bfloat16))
    solution = initial
    direction = residual
    for iteration in range(ITERS):
        mapped = apply_now(direction.astype(jnp.bfloat16))
        norm_now, curvature, cross_term, square_term = lax.psum(
            (
                local_inner(residual, residual),
                local_inner(direction, mapped),
                local_inner(residual, mapped),
                local_inner(mapped, mapped),
            ),
            ("region", "dev"),
        )
        step_length = norm_now / curvature
        solution = solution + step_length[:, None] * direction
        residual = residual - step_length[:, None] * mapped
        if iteration + 1 < ITERS:
            norm_next = (
                norm_now - 2.0 * step_length * cross_term + step_length * step_length * square_term
            )
            direction = residual + (norm_next / norm_now)[:, None] * direction
    return (solution, residual)


def solution(mesh):
    return jax.shard_map(
        per_device,
        mesh=mesh,
        in_specs=(
            P(("groups", "region", "dev"), None, None, None),
            P(("groups", "region", "dev"), None, None),
            P(("groups", "region", "dev"), None, None, None, None),
            P(("groups", "region", "dev"), None, None, None),
            P(("groups", "region", "dev"), None, None),
            P(None, ("groups", "region", "dev")),
            P(None, ("groups", "region", "dev")),
        ),
        out_specs=(P(None, ("groups", "region", "dev")), P(None, ("groups", "region", "dev"))),
        check_vma=False,
    )
```

profile of v0, /device:TPU:0, one launch (start us, length us, event | category | flops | bytes accessed | tf_op | source)
XLA Modules:
  0.0 152.3 jit_solution(10185880619438954672)
XLA Ops:
  0.6 0.8 compare_select_fusion.2
  1.6 1.3 copy_bitcast_fusion.2
  2.9 0.6 gather_fusion.1
  3.5 3.1 %collective-permute-start = (bf16[32,1,12,128]{3,0,2,1:T(8,128)(2,1)S(1)}, bf16[32,1,12,128]{3,0,2,1:T(8,128)(2,1)S(1)}, u32[]{:S(2)}, u32[]{:S(2)}) collective-permute-start(bf16[32,1,12,128]{3,0,2,1:T(8,128)(2,1)S(1)} %get-tuple-element.25), channel_id=1, source_target_pairs={{0,1},{1,2},{2,3},{3,0},{4,5},{5,6},{6,7},{7,4},{8,9},{9,10},{10,1... | collective-permute-start | bytes 294920 | tf_op jit(solution)/shard_map/ppermute | solution.py:16
  6.6 2.1 %collective-permute-start.1 = (bf16[32,1,12,128]{3,0,2,1:T(8,128)(2,1)S(1)}, bf16[32,1,12,128]{3,0,2,1:T(8,128)(2,1)S(1)}, u32[]{:S(2)}, u32[]{:S(2)}) collective-permute-start(bf16[32,1,12,128]{3,0,2,1:T(8,128)(2,1)S(1)} %get-tuple-element.26), channel_id=1, source_target_pairs={{1,0},{2,1},{3,2},{0,3},{5,4},{6,5},{7,6},{4,7},{9,8},{10,9},{11,1... | collective-permute-start | bytes 294920 | tf_op jit(solution)/shard_map/ppermute | solution.py:17
  9.5 1.7 %collective-permute-start.3 = (bf16[32,1,12,128]{3,0,2,1:T(8,128)(2,1)S(1)}, bf16[32,1,12,128]{3,0,2,1:T(8,128)(2,1)S(1)}, u32[]{:S(2)}, u32[]{:S(2)}) collective-permute-start(bf16[32,1,12,128]{3,0,2,1:T(8,128)(2,1)S(1)} %get-tuple-element.28), channel_id=1, source_target_pairs={{4,0},{8,4},{12,8},{0,12},{5,1},{9,5},{13,9},{1,13},{6,2},{10,6},{... | collective-permute-start | bytes 294920 | tf_op jit(solution)/shard_map/ppermute | solution.py:17
  11.3 2.0 %gather_fusion = bf16[192,32,128]{2,1,0:T(8,128)(2,1)} fusion(bf16[32,64,128]{2,0,1:T(8,128)(2,1)S(1)} %copy_bitcast_fusion.2, s32[1024]{0:T(1024)S(1)} %pad_clamp_fusion.6), kind=kCustom, calls=%fused_computation | custom fusion | bytes 3146496 | tf_op jit(solution)/shard_map/gather | solution.py:31
  13.4 8.3 %fusion.12 = f32[32,192,128]{2,0,1:T(8,128)} fusion(bf16[1,192,128,128]{3,2,1,0:T(8,128)(2,1)} %param.7, bf16[192,32,128]{2,1,0:T(8,128)(2,1)} %gather_fusion), kind=kOutput, calls=%fused_computation.33 | convolution fusion | flops 201326592 | bytes 11010048 | tf_op jit(solution)/shard_map/cnv,nwv->cnw/dot_general | solution.py:32
  24.0 0.9 fusion.39
  25.0 1.2 convolution_bitcast_fusion.2
  26.2 3.2 %fusion.30 = f32[64,32,128]{2,0,1:T(8,128)S(1)} fusion(f32[64,32,128]{2,0,1:T(8,128)S(1)} %convolution_bitcast_fusion.2, f32[32,192,128]{2,0,1:T(8,128)S(1)} %copy-done.4, s32[192]{0:T(256)S(1)} %bitcast.258), kind=kOutput, calls=%fused_computation.45 | convolution fusion | flops 604254208 | bytes 5243648 | tf_op jit(solution)/shard_map/cnw,nb->cbw/dot_general | solution.py:36
  29.4 0.7 convert_bitcast_fusion.1
  30.2 0.6 gather_fusion.8
  30.8 0.7 gather_fusion.11
  31.5 2.0 %gather_fusion.7 = bf16[192,32,128]{2,1,0:T(8,128)(2,1)} fusion(bf16[32,64,128]{2,0,1:T(8,128)(2,1)S(1)} %bitcast.221, s32[1024]{0:T(1024)S(1)} %pad_clamp_fusion.6), kind=kCustom, calls=%fused_computation.7 | custom fusion | bytes 3146496 | tf_op jit(solution)/shard_map/gather | solution.py:31
  33.5 0.7 fusion.100
  34.2 3.8 %collective-permute-start.5 = (bf16[32,1,12,128]{3,0,2,1:T(8,128)(2,1)}, bf16[32,1,12,128]{3,0,2,1:T(8,128)(2,1)S(1)}, u32[]{:S(2)}, u32[]{:S(2)}) collective-permute-start(bf16[32,1,12,128]{3,0,2,1:T(8,128)(2,1)} %get-tuple-element.22), channel_id=1, source_target_pairs={{1,0},{2,1},{3,2},{0,3},{5,4},{6,5},{7,6},{4,7},{9,8},{10,9},{11,1... | collective-permute-start | bytes 294920 | tf_op jit(solution)/shard_map/ppermute | solution.py:17
  38.1 1.7 %collective-permute-start.7 = (bf16[32,1,12,128]{3,0,2,1:T(8,128)(2,1)S(1)}, bf16[32,1,12,128]{3,0,2,1:T(8,128)(2,1)S(1)}, u32[]{:S(2)}, u32[]{:S(2)}) collective-permute-start(bf16[32,1,12,128]{3,0,2,1:T(8,128)(2,1)S(1)} %get-tuple-element.24), channel_id=1, source_target_pairs={{4,0},{8,4},{12,8},{0,12},{5,1},{9,5},{13,9},{1,13},{6,2},{10,6},{... | collective-permute-start | bytes 294920 | tf_op jit(solution)/shard_map/ppermute | solution.py:17
  39.8 8.3 %fusion.15 = f32[32,192,128]{2,0,1:T(8,128)} fusion(bf16[1,192,128,128]{3,2,1,0:T(8,128)(2,1)} %param.7, bf16[192,32,128]{2,1,0:T(8,128)(2,1)} %gather_fusion.7), kind=kOutput, calls=%fused_computation.34 | convolution fusion | flops 201326592 | bytes 11010048 | tf_op jit(solution)/shard_map/cnv,nwv->cnw/dot_general | solution.py:32
  48.1 0.7 gather_fusion.9
  48.8 0.7 gather_fusion.10
  49.5 0.7 gather_fusion.12
  50.2 0.7 gather_fusion.13
  50.9 0.9 fusion.42
  51.8 1.2 convolution_bitcast_fusion.1
  53.1 3.4 %fusion.52 = (f32[32]{0:T(128)S(1)}, f32[64,32,128]{2,0,1:T(8,128)S(1)}) fusion(f32[64,32,128]{2,0,1:T(8,128)S(1)} %convolution_bitcast_fusion.1, f32[32,192,128]{2,0,1:T(8,128)S(1)} %copy-done.5, s32[192]{0:T(256)S(1)} %bitcast.259), kind=kOutput, calls=%fused_computation.64 | convolution fusion | flops 604778496 | bytes 5243776 | tf_op jit(solution)/shard_map/cnw,nb->cbw/dot_general | solution.py:36
  56.5 1.0 copy-done.1
  57.5 0.8 fusion.50
  58.3 29.7 %all-reduce.1 = (f32[32]{0:T(128)S(1)}, f32[32]{0:T(128)S(1)}, f32[32]{0:T(128)S(1)}) all-reduce(f32[32]{0:T(128)S(1)} %get-tuple-element.5, f32[32]{0:T(128)S(1)} %get-tuple-element.35, f32[32]{0:T(128)S(1)} %get-tuple-element.4), channel_id=1, replica_groups=mesh['groups'=2,'region'=4,'dev'=4] {'region','dev'}, use_global_device_ids=true, to_apply=%region_1.0 | all-reduce | flops 96 | bytes 768 | tf_op jit(solution)/shard_map/psum | solution.py:76
  88.0 1.9 %copy_bitcast_fusion = bf16[32,64,128]{2,0,1:T(8,128)(2,1)S(1)} fusion(f32[32,8192]{1,0:T(8,128)S(1)} %get-tuple-element.14, f32[32]{0:T(128)S(1)} %get-tuple-element.11, f32[4,8,64,128]{3,2,1,0:T(8,128)} %bitcast.216, f32[32]{0:T(128)S(1)} %get-tuple-element.12), kind=kLoop, calls=%fused_computation.72 | loop fusion | flops 1310720 | bytes 2621696 | tf_op jit(solution)/shard_map/reshape | solution.py:28
  89.8 2.0 %gather_fusion.14 = bf16[192,32,128]{2,1,0:T(8,128)(2,1)} fusion(bf16[32,64,128]{2,0,1:T(8,128)(2,1)S(1)} %copy_bitcast_fusion, s32[1024]{0:T(1024)S(1)} %pad_clamp_fusion.6), kind=kCustom, calls=%fused_computation.14 | custom fusion | bytes 3146496 | tf_op jit(solution)/shard_map/gather | solution.py:31
  91.9 0.6 gather_fusion.15
  92.5 0.7 gather_fusion.18
  93.2 0.7 fusion.98
  93.8 2.2 %collective-permute-start.8 = (bf16[32,1,12,128]{3,0,2,1:T(8,128)(2,1)S(1)}, bf16[32,1,12,128]{3,0,2,1:T(8,128)(2,1)S(1)}, u32[]{:S(2)}, u32[]{:S(2)}) collective-permute-start(bf16[32,1,12,128]{3,0,2,1:T(8,128)(2,1)S(1)} %get-tuple-element.17), channel_id=1, source_target_pairs={{0,1},{1,2},{2,3},{3,0},{4,5},{5,6},{6,7},{7,4},{8,9},{9,10},{10,1... | collective-permute-start | bytes 294920 | tf_op jit(solution)/shard_map/ppermute | solution.py:16
  96.1 1.6 %collective-permute-start.9 = (bf16[32,1,12,128]{3,0,2,1:T(8,128)(2,1)}, bf16[32,1,12,128]{3,0,2,1:T(8,128)(2,1)S(1)}, u32[]{:S(2)}, u32[]{:S(2)}) collective-permute-start(bf16[32,1,12,128]{3,0,2,1:T(8,128)(2,1)} %get-tuple-element.18), channel_id=1, source_target_pairs={{1,0},{2,1},{3,2},{0,3},{5,4},{6,5},{7,6},{4,7},{9,8},{10,9},{11,1... | collective-permute-start | bytes 294920 | tf_op jit(solution)/shard_map/ppermute | solution.py:17
  97.7 1.8 %collective-permute-start.11 = (bf16[32,1,12,128]{3,0,2,1:T(8,128)(2,1)S(1)}, bf16[32,1,12,128]{3,0,2,1:T(8,128)(2,1)S(1)}, u32[]{:S(2)}, u32[]{:S(2)}) collective-permute-start(bf16[32,1,12,128]{3,0,2,1:T(8,128)(2,1)S(1)} %get-tuple-element.20), channel_id=1, source_target_pairs={{4,0},{8,4},{12,8},{0,12},{5,1},{9,5},{13,9},{1,13},{6,2},{10,6},{... | collective-permute-start | bytes 294920 | tf_op jit(solution)/shard_map/ppermute | solution.py:17
  99.5 8.3 %fusion.18 = f32[32,192,128]{2,0,1:T(8,128)} fusion(bf16[1,192,128,128]{3,2,1,0:T(8,128)(2,1)} %param.7, bf16[192,32,128]{2,1,0:T(8,128)(2,1)} %gather_fusion.14), kind=kOutput, calls=%fused_computation.35 | convolution fusion | flops 201326592 | bytes 11010048 | tf_op jit(solution)/shard_map/cnv,nwv->cnw/dot_general | solution.py:32
  107.8 0.7 gather_fusion.16
  108.5 0.7 gather_fusion.17
  109.2 0.7 gather_fusion.19
  109.9 0.7 gather_fusion.20
  110.6 0.9 fusion.45
  111.5 1.2 convolution_bitcast_fusion
  112.8 3.2 %fusion.36 = f32[64,32,128]{2,0,1:T(8,128)S(1)} fusion(f32[64,32,128]{2,0,1:T(8,128)S(1)} %convolution_bitcast_fusion, f32[32,192,128]{2,0,1:T(8,128)S(1)} %copy-done.3, s32[192]{0:T(256)S(1)} %bitcast.260), kind=kOutput, calls=%fused_computation.47 | convolution fusion | flops 604254208 | bytes 5243648 | tf_op jit(solution)/shard_map/cnw,nb->cbw/dot_general | solution.py:36
  116.0 1.5 fusion.48
  117.5 30.1 %all-reduce = (f32[32]{0:T(128)S(1)}, f32[32]{0:T(128)S(1)}) all-reduce(f32[32]{0:T(128)S(1)} %get-tuple-element.3, f32[32]{0:T(128)S(1)} %get-tuple-element.2), channel_id=1, replica_groups=mesh['groups'=2,'region'=4,'dev'=4] {'region','dev'}, use_global_device_ids=true, to_apply=%region_5.0 | all-reduce | flops 64 | bytes 512 | tf_op jit(solution)/shard_map/psum | solution.py:76
  147.5 4.7 %fusion.49 = (f32[32,8192]{1,0:T(8,128)}, f32[32,8192]{1,0:T(8,128)}) fusion(f32[4,8,64,128]{3,2,1,0:T(8,128)} %bitcast.223, f32[32]{0:T(128)S(1)} %div.11, f32[32,8192]{1,0:T(8,128)S(1)} %get-tuple-element.14, f32[4,8,64,128]{3,2,1,0:T(8,128)} %bitcast.217, f32[32]{0:T(128)S(1)} %copy-done.12, f32[32]{0:T(128)S(1)} %copy-done.10, f32[32,8192]{1,0:T(8,128)} %param.13), kind=kLoop, calls=%fused_computation.57 | loop fusion | flops 2621440 | bytes 6291840 | tf_op jit(solution)/shard_map/sub | solution.py:87
  (78 shorter events, 3.5 us)
Async XLA Ops:
  0.6 23.4 %copy-start = (bf16[1,4,12,128,128]{4,3,2,1,0:T(8,128)(2,1)S(1)}, bf16[1,4,12,128,128]{4,3,2,1,0:T(8,128)(2,1)}, u32[]{:S(2)}) copy-start(bf16[1,4,12,128,128]{4,3,2,1,0:T(8,128)(2,1)} %param.9) | copy-start | bytes 4718596
  1.6 9.6 %copy-start.17 = (s32[1,4,2,12]{3,2,1,0:T(2,128)S(1)}, s32[1,4,2,12]{3,2,1,0:T(2,128)}, u32[]{:S(2)}) copy-start(s32[1,4,2,12]{3,2,1,0:T(2,128)} %param.10) | copy-start | bytes 1156
  1.6 9.7 %copy-start.18 = (s32[1,2,192]{2,1,0:T(2,128)S(1)}, s32[1,2,192]{2,1,0:T(2,128)}, u32[]{:S(2)}) copy-start(s32[1,2,192]{2,1,0:T(2,128)} %param.8) | copy-start | bytes 4612
  3.5 18.1 %collective-permute-start = (bf16[32,1,12,128]{3,0,2,1:T(8,128)(2,1)S(1)}, bf16[32,1,12,128]{3,0,2,1:T(8,128)(2,1)S(1)}, u32[]{:S(2)}, u32[]{:S(2)}) collective-permute-start(bf16[32,1,12,128]{3,0,2,1:T(8,128)(2,1)S(1)} %get-tuple-element.25), channel_id=1, source_target_pairs={{0,1},{1,2},{2,3},{3,0},{4,5},{5,6},{6,7},{7,4},{8,9},{9,10},{10,1... | collective-permute-start | bytes 294920 | tf_op jit(solution)/shard_map/ppermute | solution.py:16
  6.6 15.7 %collective-permute-start.1 = (bf16[32,1,12,128]{3,0,2,1:T(8,128)(2,1)S(1)}, bf16[32,1,12,128]{3,0,2,1:T(8,128)(2,1)S(1)}, u32[]{:S(2)}, u32[]{:S(2)}) collective-permute-start(bf16[32,1,12,128]{3,0,2,1:T(8,128)(2,1)S(1)} %get-tuple-element.26), channel_id=1, source_target_pairs={{1,0},{2,1},{3,2},{0,3},{5,4},{6,5},{7,6},{4,7},{9,8},{10,9},{11,1... | collective-permute-start | bytes 294920 | tf_op jit(solution)/shard_map/ppermute | solution.py:17
  8.8 0.6 copy-start.8
  9.4 13.5 %collective-permute-start.2 = (bf16[32,1,12,128]{3,0,2,1:T(8,128)(2,1)S(1)}, bf16[32,1,12,128]{3,0,2,1:T(8,128)(2,1)S(1)}, u32[]{:S(2)}, u32[]{:S(2)}) collective-permute-start(bf16[32,1,12,128]{3,0,2,1:T(8,128)(2,1)S(1)} %get-tuple-element.27), channel_id=1, source_target_pairs={{0,4},{4,8},{8,12},{12,0},{1,5},{5,9},{9,13},{13,1},{2,6},{6,10},{... | collective-permute-start | bytes 294920 | tf_op jit(solution)/shard_map/ppermute | solution.py:16
  9.5 14.0 %collective-permute-start.3 = (bf16[32,1,12,128]{3,0,2,1:T(8,128)(2,1)S(1)}, bf16[32,1,12,128]{3,0,2,1:T(8,128)(2,1)S(1)}, u32[]{:S(2)}, u32[]{:S(2)}) collective-permute-start(bf16[32,1,12,128]{3,0,2,1:T(8,128)(2,1)S(1)} %get-tuple-element.28), channel_id=1, source_target_pairs={{4,0},{8,4},{12,8},{0,12},{5,1},{9,5},{13,9},{1,13},{6,2},{10,6},{... | collective-permute-start | bytes 294920 | tf_op jit(solution)/shard_map/ppermute | solution.py:17
  11.3 10.4 %copy-start.16 = (s32[1024]{0:T(1024)}, s32[1024]{0:T(1024)S(1)}, u32[]{:S(2)}) copy-start(s32[1024]{0:T(1024)S(1)} %pad_clamp_fusion.4) | copy-start | bytes 12292
  11.3 11.0 %copy-start.15 = (s32[1024]{0:T(1024)}, s32[1024]{0:T(1024)S(1)}, u32[]{:S(2)}) copy-start(s32[1024]{0:T(1024)S(1)} %pad_clamp_fusion.3) | copy-start | bytes 12292
  11.3 11.5 %copy-start.13 = (s32[1024]{0:T(1024)}, s32[1024]{0:T(1024)S(1)}, u32[]{:S(2)}) copy-start(s32[1024]{0:T(1024)S(1)} %pad_clamp_fusion.1) | copy-start | bytes 12292
  21.6 3.3 %copy-start.14 = (s32[1024]{0:T(1024)}, s32[1024]{0:T(1024)S(1)}, u32[]{:S(2)}) copy-start(s32[1024]{0:T(1024)S(1)} %pad_clamp_fusion) | copy-start | bytes 12292
  24.0 2.1 %copy-start.4 = (f32[32,192,128]{2,0,1:T(8,128)S(1)}, f32[32,192,128]{2,0,1:T(8,128)}, u32[]{:S(2)}) copy-start(f32[32,192,128]{2,0,1:T(8,128)} %fusion.12) | copy-start | bytes 9437188
  26.2 3.2 %copy-start.7 = (f32[32,8192]{1,0:T(8,128)S(1)}, f32[32,8192]{1,0:T(8,128)}, u32[]{:S(2)}) copy-start(f32[32,8192]{1,0:T(8,128)} %param.12) | copy-start | bytes 3145732
  34.2 13.9 %collective-permute-start.4 = (bf16[32,1,12,128]{3,0,2,1:T(8,128)(2,1)S(1)}, bf16[32,1,12,128]{3,0,2,1:T(8,128)(2,1)S(1)}, u32[]{:S(2)}, u32[]{:S(2)}) collective-permute-start(bf16[32,1,12,128]{3,0,2,1:T(8,128)(2,1)S(1)} %get-tuple-element.21), channel_id=1, source_target_pairs={{0,1},{1,2},{2,3},{3,0},{4,5},{5,6},{6,7},{7,4},{8,9},{9,10},{10,1... | collective-permute-start | bytes 294920 | tf_op jit(solution)/shard_map/ppermute | solution.py:16
  34.2 14.6 %collective-permute-start.5 = (bf16[32,1,12,128]{3,0,2,1:T(8,128)(2,1)}, bf16[32,1,12,128]{3,0,2,1:T(8,128)(2,1)S(1)}, u32[]{:S(2)}, u32[]{:S(2)}) collective-permute-start(bf16[32,1,12,128]{3,0,2,1:T(8,128)(2,1)} %get-tuple-element.22), channel_id=1, source_target_pairs={{1,0},{2,1},{3,2},{0,3},{5,4},{6,5},{7,6},{4,7},{9,8},{10,9},{11,1... | collective-permute-start | bytes 294920 | tf_op jit(solution)/shard_map/ppermute | solution.py:17
  38.0 11.5 %collective-permute-start.6 = (bf16[32,1,12,128]{3,0,2,1:T(8,128)(2,1)S(1)}, bf16[32,1,12,128]{3,0,2,1:T(8,128)(2,1)S(1)}, u32[]{:S(2)}, u32[]{:S(2)}) collective-permute-start(bf16[32,1,12,128]{3,0,2,1:T(8,128)(2,1)S(1)} %get-tuple-element.23), channel_id=1, source_target_pairs={{0,4},{4,8},{8,12},{12,0},{1,5},{5,9},{9,13},{13,1},{2,6},{6,10},{... | collective-permute-start | bytes 294920 | tf_op jit(solution)/shard_map/ppermute | solution.py:16
  38.1 12.1 %collective-permute-start.7 = (bf16[32,1,12,128]{3,0,2,1:T(8,128)(2,1)S(1)}, bf16[32,1,12,128]{3,0,2,1:T(8,128)(2,1)S(1)}, u32[]{:S(2)}, u32[]{:S(2)}) collective-permute-start(bf16[32,1,12,128]{3,0,2,1:T(8,128)(2,1)S(1)} %get-tuple-element.24), channel_id=1, source_target_pairs={{4,0},{8,4},{12,8},{0,12},{5,1},{9,5},{13,9},{1,13},{6,2},{10,6},{... | collective-permute-start | bytes 294920 | tf_op jit(solution)/shard_map/ppermute | solution.py:17
  50.9 2.1 %copy-start.5 = (f32[32,192,128]{2,0,1:T(8,128)S(1)}, f32[32,192,128]{2,0,1:T(8,128)}, u32[]{:S(2)}) copy-start(f32[32,192,128]{2,0,1:T(8,128)} %fusion.15) | copy-start | bytes 9437188
  56.5 1.0 copy-start.1
  88.0 3.9 %copy-start.9 = (f32[32]{0:T(128)}, f32[32]{0:T(128)S(1)}, u32[]{:S(2)}) copy-start(f32[32]{0:T(128)S(1)} %get-tuple-element.11) | copy-start | bytes 388
  88.0 3.9 %copy-start.11 = (f32[32]{0:T(128)}, f32[32]{0:T(128)S(1)}, u32[]{:S(2)}) copy-start(f32[32]{0:T(128)S(1)} %get-tuple-element.12) | copy-start | bytes 388
  93.8 13.9 %collective-permute-start.8 = (bf16[32,1,12,128]{3,0,2,1:T(8,128)(2,1)S(1)}, bf16[32,1,12,128]{3,0,2,1:T(8,128)(2,1)S(1)}, u32[]{:S(2)}, u32[]{:S(2)}) collective-permute-start(bf16[32,1,12,128]{3,0,2,1:T(8,128)(2,1)S(1)} %get-tuple-element.17), channel_id=1, source_target_pairs={{0,1},{1,2},{2,3},{3,0},{4,5},{5,6},{6,7},{7,4},{8,9},{9,10},{10,1... | collective-permute-start | bytes 294920 | tf_op jit(solution)/shard_map/ppermute | solution.py:16
  96.1 12.4 %collective-permute-start.9 = (bf16[32,1,12,128]{3,0,2,1:T(8,128)(2,1)}, bf16[32,1,12,128]{3,0,2,1:T(8,128)(2,1)S(1)}, u32[]{:S(2)}, u32[]{:S(2)}) collective-permute-start(bf16[32,1,12,128]{3,0,2,1:T(8,128)(2,1)} %get-tuple-element.18), channel_id=1, source_target_pairs={{1,0},{2,1},{3,2},{0,3},{5,4},{6,5},{7,6},{4,7},{9,8},{10,9},{11,1... | collective-permute-start | bytes 294920 | tf_op jit(solution)/shard_map/ppermute | solution.py:17
  97.7 11.5 %collective-permute-start.10 = (bf16[32,1,12,128]{3,0,2,1:T(8,128)(2,1)S(1)}, bf16[32,1,12,128]{3,0,2,1:T(8,128)(2,1)S(1)}, u32[]{:S(2)}, u32[]{:S(2)}) collective-permute-start(bf16[32,1,12,128]{3,0,2,1:T(8,128)(2,1)S(1)} %get-tuple-element.19), channel_id=1, source_target_pairs={{0,4},{4,8},{8,12},{12,0},{1,5},{5,9},{9,13},{13,1},{2,6},{6,10},{... | collective-permute-start | bytes 294920 | tf_op jit(solution)/shard_map/ppermute | solution.py:16
  97.7 12.1 %collective-permute-start.11 = (bf16[32,1,12,128]{3,0,2,1:T(8,128)(2,1)S(1)}, bf16[32,1,12,128]{3,0,2,1:T(8,128)(2,1)S(1)}, u32[]{:S(2)}, u32[]{:S(2)}) collective-permute-start(bf16[32,1,12,128]{3,0,2,1:T(8,128)(2,1)S(1)} %get-tuple-element.20), channel_id=1, source_target_pairs={{4,0},{8,4},{12,8},{0,12},{5,1},{9,5},{13,9},{1,13},{6,2},{10,6},{... | collective-permute-start | bytes 294920 | tf_op jit(solution)/shard_map/ppermute | solution.py:17
  110.6 2.1 %copy-start.3 = (f32[32,192,128]{2,0,1:T(8,128)S(1)}, f32[32,192,128]{2,0,1:T(8,128)}, u32[]{:S(2)}) copy-start(f32[32,192,128]{2,0,1:T(8,128)} %fusion.18) | copy-start | bytes 9437188
  112.7 3.2 %copy-start.2 = (f32[64,32,128]{2,0,1:T(8,128)S(1)}, f32[64,32,128]{2,0,1:T(8,128)}, u32[]{:S(2)}) copy-start(f32[64,32,128]{2,0,1:T(8,128)} %copy-done.1) | copy-start | bytes 3145732
  112.8 3.2 %copy-start.10 = (f32[32]{0:T(128)S(1)}, f32[32]{0:T(128)}, u32[]{:S(2)}) copy-start(f32[32]{0:T(128)} %copy-done.9) | copy-start | bytes 388
  112.8 3.2 %copy-start.12 = (f32[32]{0:T(128)S(1)}, f32[32]{0:T(128)}, u32[]{:S(2)}) copy-start(f32[32]{0:T(128)} %copy-done.11) | copy-start | bytes 388
  115.9 1.5 copy-start.6
where the time goes:
time: 153 us; the launch traced here: 152 us
  blocking collectives  59.8 us (39%)
  matrix products  41 us (27%)
  local copies, waits for them, and re-layouts  20.3 us (13%)
  starting transfers between devices  18.2 us (12%)
  other arithmetic  11.8 us (8%)
    psum x2, blocking collectives, per_device(): lax.psum((local_inner(residual, residual), local_inner(direction, mapped)...  59.8 us
    dot_general x3, matrix products, apply_precision(): jnp.einsum('cnv,nwv->cnw', picked, inner_blocks[0], preferred_element_typ...  24.8 us
    ppermute x6, starting transfers between devices, padded(): after = lax.ppermute(first, axis, down)  12.7 us
    dot_general x3, matrix products, apply_precision(): jnp.einsum('cnw,nb->cbw', product, placing, precision=lax.Precision.HIGHEST)  9.76 us
    gather x12, local copies, waits for them, and re-layouts, apply_precision(): received[heading][:, slot_index[heading]]  7.75 us
    gather x3, local copies, waits for them, and re-layouts, apply_precision(): picked = block_view[:, inner_cols]  6.08 us
    ppermute x6, starting transfers between devices, padded(): before = lax.ppermute(last, axis, up)  5.49 us
    sub x1, other arithmetic, per_device(): residual = residual - step_length[:, None] * mapped  4.75 us
  transfers between devices with their start and end apart: 12, of which 0 were waited for; matrix products, arithmetic and copies ran while one was open for 22% of the time, Pallas kernels for 0%

commit v1 on v0

v1 whole, which is shorter than its diff:
```python
import functools

import jax
import jax.numpy as jnp
from jax import lax
from jax.experimental import pallas as pl
from jax.experimental.pallas import tpu as pltpu
from jax.sharding import PartitionSpec as P

MESH = pl.DeviceIdType.MESH
ITERS = 2
F32 = jnp.float32
I32 = jnp.int32


def to_sublanes(values, square):
    return jnp.sum(jnp.where(square, values, 0), axis=1, keepdims=True)


def sort_tables(row_lane, col_lane, length):
    lane = lax.broadcasted_iota(I32, (length, length), 1)
    sub = lax.broadcasted_iota(I32, (length, length), 0)
    eye = lane == sub
    key_lane = row_lane * 256 + lax.broadcasted_iota(I32, (1, length), 1)
    key_sub = to_sublanes(key_lane, eye)
    row_sub = to_sublanes(row_lane, eye)
    col_sub = to_sublanes(col_lane, eye)
    rank = jnp.sum(jnp.where(key_lane < key_sub, 1, 0), axis=1, keepdims=True)
    less = jnp.sum(jnp.where(row_lane < row_sub, 1, 0), axis=1, keepdims=True)
    keep = jnp.where(rank == less, 0, 1)
    packed = (key_sub - row_sub * 256) + keep * 256 + col_sub * 512
    order = jnp.sum(jnp.where(rank == lane, packed, 0), axis=0, keepdims=True)
    upto = jnp.sum(jnp.where(row_sub <= lane, 1, 0), axis=0, keepdims=True)
    count = jnp.sum(jnp.where(row_sub == lane, 1, 0), axis=0, keepdims=True)
    return order, upto - 1, count


def kernel(
    nr, nd, inner_hbm, ipat, bnd_hbm, bpat, send_list, rhs_hbm, init_hbm, x_hbm, r_hbm,
    q, qb, x, r, w, d, v, run, runb, prodb, out_box, tab, tab_s, part, slots,
    local_sem, out_sem, in_sem, red_out, red_in, *in_box,
):
    n_inner = q.shape[0]
    halo = out_box.shape[2]
    n_bnd = 4 * halo
    blocks = v.shape[0]
    chains = v.shape[1]
    n_all = nr * nd
    region, dev = lax.axis_index("region"), lax.axis_index("dev")
    me = region * nd + dev

    chunk = n_inner // 4
    loads = [pltpu.make_async_copy(init_hbm, x, local_sem.at[0])]
    for i in range(4):
        part_of = pl.ds(i * chunk, chunk)
        loads.append(pltpu.make_async_copy(inner_hbm.at[0, part_of], q.at[part_of], local_sem.at[1 + i]))
    loads.append(pltpu.make_async_copy(bnd_hbm.at[0], qb, local_sem.at[5]))
    loads.append(pltpu.make_async_copy(rhs_hbm, r, local_sem.at[6]))
    for load in loads:
        load.start()

    def greet(t, _):
        peer = lax.rem(me + t, n_all)
        pl.semaphore_signal(
            barrier, inc=1, device_id={"region": peer // nd, "dev": lax.rem(peer, nd)}, device_id_type=MESH
        )
        return 0

    barrier = pltpu.get_barrier_semaphore()
    lax.fori_loop(1, n_all, greet, 0)

    order, last, count = sort_tables(ipat[0, 1:2, :], ipat[0, 0:1, :], n_inner)
    tab[0:1, 0:n_inner] = order
    tab[1:2, 0:n_inner] = jnp.where(count > 0, last, n_inner)
    lane128 = lax.broadcasted_iota(I32, (1, 128), 1)
    brow = jnp.full((1, 128), 1 << 20, I32)
    for k in range(4):
        for e in range(halo):
            brow = jnp.where(lane128 == k * halo + e, bpat[0, k, 0, e], brow)
    order, last, count = sort_tables(brow, jnp.zeros((1, 128), I32), 128)
    tab[2:3, 0:128] = order
    tab[3:4, 0:128] = jnp.where(count > 0, last, n_bnd)
    tables = pltpu.make_async_copy(tab, tab_s, local_sem.at[7])
    tables.start()
    run[n_inner] = jnp.zeros((chains, 128), F32)
    runb[n_bnd] = jnp.zeros((chains, 128), F32)

    targets = (
        {"dev": lax.rem(dev + nd - 1, nd)},
        {"dev": lax.rem(dev + 1, nd)},
        {"region": lax.rem(region + nr - 1, nr)},
        {"region": lax.rem(region + 1, nr)},
    )
    arrives_at = (1, 0, 3, 2)

    def cols(b):
        return pl.ds(pl.multiple_of(b * 128, 128), 128)

    def box_copy(turn, k):
        return pltpu.make_async_remote_copy(
            src_ref=out_box.at[turn, k],
            dst_ref=in_box[turn * 4 + arrives_at[k]],
            send_sem=out_sem.at[turn, k],
            recv_sem=in_sem.at[turn, arrives_at[k]],
            device_id=targets[k],
            device_id_type=MESH,
        )

    def send_halo(turn):
        for k in (0, 1, 2, 3):
            for e in range(halo):
                out_box[turn, k, e] = v[send_list[0, k, e]]
            box_copy(turn, k).start()

    def apply_parts(turn):
        def inner_step(s, acc):
            word = tab_s[0, s]
            entry, keep, col = word & 255, (word >> 8) & 1, word >> 9
            product = jnp.dot(v[col], q[entry], preferred_element_type=F32)
            acc = jnp.where(jnp.full((chains, 128), keep) != 0, acc, 0.0) + product
            run[s] = acc
            return acc

        lax.fori_loop(0, n_inner, inner_step, jnp.zeros((chains, 128), F32), unroll=8)
        for k in (2, 3, 0, 1):
            box_copy(turn, arrives_at[k]).wait_recv()

            def far_step(e, _):
                prodb[k * halo + e] = lax.dot_general(
                    in_box[turn * 4 + k][bpat[0, k, 1, e]],
                    qb[k, e],
                    (((1,), (1,)), ((), ())),
                    preferred_element_type=F32,
                )
                return 0

            lax.fori_loop(0, halo, far_step, 0, unroll=True)

        def gather_step(s, acc):
            word = tab_s[2, s]
            entry, keep = word & 255, (word >> 8) & 1
            acc = jnp.where(jnp.full((chains, 128), keep) != 0, acc, 0.0) + prodb[entry]
            runb[s] = acc
            return acc

        lax.fori_loop(0, n_bnd, gather_step, jnp.zeros((chains, 128), F32), unroll=8)

    def mapped_of(b):
        return run[tab_s[1, b]] + runb[tab_s[3, b]]

    chain = lax.broadcasted_iota(I32, (chains, 128), 0)
    lane = lax.broadcasted_iota(I32, (chains, 128), 1)

    def all_sum(turn, sums):
        packed = jnp.zeros((chains, 128), F32)
        for j, value in enumerate(sums):
            packed = packed + jnp.where(
                lane == chain + j * chains, jnp.sum(value, axis=1, keepdims=True), 0.0
            )
        row = jnp.sum(packed, axis=0, keepdims=True)
        part[turn] = row
        slots[turn, me] = row

        def copy_to(t):
            peer = lax.rem(me + t, n_all)
            return pltpu.make_async_remote_copy(
                src_ref=part.at[turn],
                dst_ref=slots.at[turn, me],
                send_sem=red_out.at[turn, peer],
                recv_sem=red_in.at[turn, me],
                device_id={"region": peer // nd, "dev": lax.rem(peer, nd)},
                device_id_type=MESH,
            )

        def copy_from(t):
            peer = lax.rem(me + t, n_all)
            return pltpu.make_async_remote_copy(
                src_ref=part.at[turn],
                dst_ref=slots.at[turn, peer],
                send_sem=red_out.at[turn, peer],
                recv_sem=red_in.at[turn, peer],
                device_id={"region": peer // nd, "dev": lax.rem(peer, nd)},
                device_id_type=MESH,
            )

        def start(t, _):
            copy_to(t).start()
            return 0

        def finish(t, _):
            copy_from(t).wait()
            return 0

        lax.fori_loop(1, n_all, start, 0)
        lax.fori_loop(1, n_all, finish, 0)
        total = jnp.sum(slots[turn].reshape(n_all, 128), axis=0, keepdims=True)
        return [
            jnp.sum(jnp.where(lane == chain + j * chains, total, 0.0), axis=1, keepdims=True)
            for j in range(len(sums))
        ]

    zero = jnp.zeros((chains, 128), F32)

    loads[0].wait()

    def round_step(b, _):
        v[b] = x[:, cols(b)].astype(jnp.bfloat16)
        return 0

    lax.fori_loop(0, blocks, round_step, 0, unroll=4)
    pl.semaphore_wait(barrier, n_all - 1)
    send_halo(0)
    tables.wait()
    for load in loads[1:]:
        load.wait()
    apply_parts(0)

    def first_step(b, rr):
        value = r[:, cols(b)] - mapped_of(b)
        r[:, cols(b)] = value
        v[b] = value.astype(jnp.bfloat16)
        return rr + value * value

    rr = lax.fori_loop(0, blocks, first_step, zero, unroll=4)

    send_halo(1)
    apply_parts(1)

    def dots_step(b, sums):
        value = mapped_of(b)
        res = r[:, cols(b)]
        w[:, cols(b)] = value
        return sums[0] + res * value, sums[1] + value * value

    rw, ww = lax.fori_loop(0, blocks, dots_step, (zero, zero), unroll=4)
    norm, cross, square = all_sum(0, (rr, rw, ww))
    step = norm / cross
    norm_next = norm - 2.0 * step * cross + step * step * square
    ratio = norm_next / norm
    step_b = jnp.broadcast_to(step, (chains, 128))
    ratio_b = jnp.broadcast_to(ratio, (chains, 128))

    def update_step(b, rr):
        old = r[:, cols(b)]
        value = old - step_b * w[:, cols(b)]
        along = value + ratio_b * old
        x[:, cols(b)] = x[:, cols(b)] + step_b * old
        r[:, cols(b)] = value
        d[:, cols(b)] = along
        v[b] = along.astype(jnp.bfloat16)
        return rr + value * value

    rr = lax.fori_loop(0, blocks, update_step, zero, unroll=4)

    send_halo(2)
    apply_parts(2)

    def last_dot_step(b, total):
        value = mapped_of(b)
        w[:, cols(b)] = value
        return total + d[:, cols(b)] * value

    dw = lax.fori_loop(0, blocks, last_dot_step, zero, unroll=4)
    norm, curve = all_sum(1, (rr, dw))
    step_c = jnp.broadcast_to(norm / curve, (chains, 128))

    def end_step(b, _):
        x[:, cols(b)] = x[:, cols(b)] + step_c * d[:, cols(b)]
        r[:, cols(b)] = r[:, cols(b)] - step_c * w[:, cols(b)]
        return 0

    lax.fori_loop(0, blocks, end_step, 0, unroll=4)
    stores = [
        pltpu.make_async_copy(x, x_hbm, local_sem.at[8]),
        pltpu.make_async_copy(r, r_hbm, local_sem.at[9]),
    ]
    for store in stores:
        store.start()
    for turn in range(3):
        for k in range(4):
            box_copy(turn, k).wait_send()
    for store in stores:
        store.wait()


def per_device(nr, nd, inner_blocks, inner_pattern, boundary_blocks, boundary_pattern, send_list, right_side, initial):
    n_inner, blk = inner_blocks.shape[1], inner_blocks.shape[2]
    halo = send_list.shape[2]
    chains, nodes = right_side.shape
    blocks = nodes // blk
    n_all = nr * nd
    anywhere = pl.BlockSpec(memory_space=pl.ANY)
    smem = pl.BlockSpec(memory_space=pltpu.SMEM)
    vmem = pl.BlockSpec(memory_space=pltpu.VMEM)
    vector = pltpu.VMEM((chains, nodes), F32)
    return pl.pallas_call(
        functools.partial(kernel, nr, nd),
        out_shape=(
            jax.ShapeDtypeStruct((chains, nodes), F32),
            jax.ShapeDtypeStruct((chains, nodes), F32),
        ),
        in_specs=[anywhere, vmem, anywhere, smem, smem, anywhere, anywhere],
        out_specs=(anywhere, anywhere),
        scratch_shapes=[
            pltpu.VMEM((n_inner, blk, blk), jnp.bfloat16),
            pltpu.VMEM((4, halo, blk, blk), jnp.bfloat16),
            vector,
            vector,
            vector,
            vector,
            pltpu.VMEM((blocks, chains, blk), jnp.bfloat16),
            pltpu.VMEM((n_inner + 1, chains, blk), F32),
            pltpu.VMEM((4 * halo + 1, chains, blk), F32),
            pltpu.VMEM((4 * halo, chains, blk), F32),
            pltpu.VMEM((3, 4, halo, chains, blk), jnp.bfloat16),
            pltpu.VMEM((8, 256), I32),
            pltpu.SMEM((8, 256), I32),
            pltpu.VMEM((ITERS, 1, 128), F32),
            pltpu.VMEM((ITERS, n_all, 1, 128), F32),
            pltpu.SemaphoreType.DMA((10,)),
            pltpu.SemaphoreType.DMA((3, 4)),
            pltpu.SemaphoreType.DMA((3, 4)),
            pltpu.SemaphoreType.DMA((ITERS, n_all)),
            pltpu.SemaphoreType.DMA((ITERS, n_all)),
        ]
        + [pltpu.VMEM((halo, chains, blk), jnp.bfloat16)] * 12,
        compiler_params=pltpu.CompilerParams(
            collective_id=0, has_side_effects=True, vmem_limit_bytes=48 * 1024 * 1024
        ),
    )(inner_blocks, inner_pattern, boundary_blocks, boundary_pattern, send_list, right_side, initial)


def solution(mesh):
    spread = ("groups", "region", "dev")
    return jax.shard_map(
        functools.partial(per_device, mesh.shape["region"], mesh.shape["dev"]),
        mesh=mesh,
        in_specs=(
            P(spread, None, None, None),
            P(spread, None, None),
            P(spread, None, None, None, None),
            P(spread, None, None, None),
            P(spread, None, None),
            P(None, spread),
            P(None, spread),
        ),
        out_specs=(P(None, spread), P(None, spread)),
        check_vma=False,
    )
```

time: 153 us -> 48 us (0.31)
  blocking collectives: 59.8 us -> 0 us
  matrix products: 41 us -> 0 us
  Pallas kernels: 0 us -> 39.2 us
  starting transfers between devices: 18.2 us -> 0 us
  local copies, waits for them, and re-layouts: 20.3 us -> 7.84 us
  other arithmetic: 11.8 us -> 0 us
    psum x2 -> x0, blocking collectives: 59.8 us -> none  [per_device(): lax.psum((local_inner(residual, residual), local_inner(direction, mapped)...]
    dot_general x12 -> x0, matrix products: 41 us -> none  [the longest x3 24.8 us: apply_precision(): jnp.einsum('cnv,nwv->cnw', picked, inner_blocks[0], preferred_element_typ...]
    pallas_call x0 -> x1, Pallas kernels: none -> 39.2 us  [per_device(): pl.pallas_call(functools.partial(kernel, nr, nd), out_shape=(jax.ShapeDty...]
    ppermute x12 -> x0, starting transfers between devices: 18.2 us -> none  [the longest x6 12.7 us: padded(): after = lax.ppermute(first, axis, down)]
    gather x21 -> x0, local copies, waits for them, and re-layouts: 17.6 us -> none  [the longest x12 7.75 us: apply_precision(): received[heading][:, slot_index[heading]]]
    unnamed x38 -> x14, local copies, waits for them, and re-layouts: 1.08 us -> 7.84 us
    sub x1 -> x0, other arithmetic: 4.75 us -> none  [per_device(): residual = residual - step_length[:, None] * mapped]
    reshape x2 -> x0, other arithmetic: 3.19 us -> none  [apply_precision(): block_view = vector.reshape(chains, block_count, block_size)]
  transfers between devices with their start and end apart: 12 -> 0, of which waited for: 0 -> 0; matrix products, arithmetic and copies ran while one was open for 22% -> 0% of each run, Pallas kernels for 0% -> 0%
where the time goes in v1:
time: 48 us; the launch traced here: 47.7 us
  Pallas kernels  39.2 us (82%)
  local copies, waits for them, and re-layouts  7.84 us (16%)
  between operations  0.65 us (1%)
    pallas_call x1, Pallas kernels, per_device(): pl.pallas_call(functools.partial(kernel, nr, nd), out_shape=(jax.ShapeDty...  39.2 us
    unnamed x14, local copies, waits for them, and re-layouts  7.84 us

profile of v1, /device:TPU:0, one launch (start us, length us, event | category | flops | bytes accessed | tf_op | source)
XLA Modules:
  0.0 47.7 jit_solution(161148431187127399)
XLA Ops:
  0.6 0.0 copy-start
  0.6 1.4 %copy-done = bf16[1,4,12,128,128]{4,3,2,1,0:T(8,128)(2,1)S(1)} copy-done((bf16[1,4,12,128,128]{4,3,2,1,0:T(8,128)(2,1)S(1)}, bf16[1,4,12,128,128]{4,3,2,1,0:T(8,128)(2,1)}, u32[]{:S(2)}) %copy-start) | copy-done | bytes 1572888
  2.0 0.0 copy-start.1
  2.0 1.2 %copy-done.1 = f32[32,8192]{1,0:T(8,128)S(1)} copy-done((f32[32,8192]{1,0:T(8,128)S(1)}, f32[32,8192]{1,0:T(8,128)}, u32[]{:S(2)}) %copy-start.1) | copy-done | bytes 1048600
  3.3 0.0 copy-start.2
  3.3 1.2 %copy-done.2 = f32[32,8192]{1,0:T(8,128)S(1)} copy-done((f32[32,8192]{1,0:T(8,128)S(1)}, f32[32,8192]{1,0:T(8,128)}, u32[]{:S(2)}) %copy-start.2) | copy-done | bytes 1048600
  4.5 0.0 copy-start.3
  4.5 0.7 %copy-done.3 = s32[1,4,2,12]{3,2,1,0:T(2,128)S(1)} copy-done((s32[1,4,2,12]{3,2,1,0:T(2,128)S(1)}, s32[1,4,2,12]{3,2,1,0:T(2,128)}, u32[]{:S(2)}) %copy-start.3) | copy-done | bytes 408
  5.2 0.0 copy-start.4
  5.2 0.7 %copy-done.4 = s32[1,2,192]{2,1,0:T(2,128)S(1)} copy-done((s32[1,2,192]{2,1,0:T(2,128)S(1)}, s32[1,2,192]{2,1,0:T(2,128)}, u32[]{:S(2)}) %copy-start.4) | copy-done | bytes 1560
  5.9 0.0 copy-start.5
  5.9 0.7 %copy-done.5 = s32[1,4,12]{2,1,0:T(4,128)S(1)} copy-done((s32[1,4,12]{2,1,0:T(4,128)S(1)}, s32[1,4,12]{2,1,0:T(4,128)}, u32[]{:S(2)}) %copy-start.5) | copy-done | bytes 216
  6.5 39.2 %shard_map.86 = (f32[32,8192]{1,0:T(8,128)S(1)}, f32[32,8192]{1,0:T(8,128)S(1)}) custom-call(bf16[1,192,128,128]{3,2,1,0:T(8,128)(2,1)} %inner_hbm.1, s32[1,2,192]{2,1,0:T(2,128)S(1)} %copy-done.4, bf16[1,4,12,128,128]{4,3,2,1,0:T(8,128)(2,1)S(1)} %copy-done, s32[1,4,2,12]{3,2,1,0:T(2,128)S(1)} %copy-done.3, s32[1,4,12]{2,1,0:T(4,128)S(1)} %copy-done.5, ...), custom_call_target="tpu_custom_call" | custom-call | tf_op jit(solution)/shard_map/pallas_call | solution.py:296
  45.8 1.0 %copy.11 = f32[32,8192]{1,0:T(8,128)} copy(f32[32,8192]{1,0:T(8,128)S(1)} %get-tuple-element.4) | data formatting | bytes 2097152
  46.7 1.0 %copy.12 = f32[32,8192]{1,0:T(8,128)} copy(f32[32,8192]{1,0:T(8,128)S(1)} %get-tuple-element.5) | data formatting | bytes 2097152
Async XLA Ops:
  0.6 1.4 %copy-start = (bf16[1,4,12,128,128]{4,3,2,1,0:T(8,128)(2,1)S(1)}, bf16[1,4,12,128,128]{4,3,2,1,0:T(8,128)(2,1)}, u32[]{:S(2)}) copy-start(bf16[1,4,12,128,128]{4,3,2,1,0:T(8,128)(2,1)} %bnd_hbm.1) | copy-start | bytes 4718596
  2.0 1.2 %copy-start.1 = (f32[32,8192]{1,0:T(8,128)S(1)}, f32[32,8192]{1,0:T(8,128)}, u32[]{:S(2)}) copy-start(f32[32,8192]{1,0:T(8,128)} %rhs_hbm.1) | copy-start | bytes 3145732
  3.3 1.2 %copy-start.2 = (f32[32,8192]{1,0:T(8,128)S(1)}, f32[32,8192]{1,0:T(8,128)}, u32[]{:S(2)}) copy-start(f32[32,8192]{1,0:T(8,128)} %init_hbm.1) | copy-start | bytes 3145732
  4.5 0.7 %copy-start.3 = (s32[1,4,2,12]{3,2,1,0:T(2,128)S(1)}, s32[1,4,2,12]{3,2,1,0:T(2,128)}, u32[]{:S(2)}) copy-start(s32[1,4,2,12]{3,2,1,0:T(2,128)} %bpat.1) | copy-start | bytes 1156
  5.2 0.7 %copy-start.4 = (s32[1,2,192]{2,1,0:T(2,128)S(1)}, s32[1,2,192]{2,1,0:T(2,128)}, u32[]{:S(2)}) copy-start(s32[1,2,192]{2,1,0:T(2,128)} %ipat.1) | copy-start | bytes 4612
  5.9 0.7 %copy-start.5 = (s32[1,4,12]{2,1,0:T(4,128)S(1)}, s32[1,4,12]{2,1,0:T(4,128)}, u32[]{:S(2)}) copy-start(s32[1,4,12]{2,1,0:T(4,128)} %send_list.1) | copy-start | bytes 580

commit v2 on v1

v2 whole, which is shorter than its diff:
```python
import functools

import jax
import jax.numpy as jnp
from jax import lax
from jax.experimental import pallas as pl
from jax.experimental.pallas import tpu as pltpu
from jax.sharding import PartitionSpec as P

MESH = pl.DeviceIdType.MESH
ITERS = 2
F32 = jnp.float32
I32 = jnp.int32


def to_sublanes(values, square):
    return jnp.sum(jnp.where(square, values, 0), axis=1, keepdims=True)


def sort_tables(row_lane, col_lane, length):
    lane = lax.broadcasted_iota(I32, (length, length), 1)
    sub = lax.broadcasted_iota(I32, (length, length), 0)
    eye = lane == sub
    key_lane = row_lane * 256 + lax.broadcasted_iota(I32, (1, length), 1)
    key_sub = to_sublanes(key_lane, eye)
    row_sub = to_sublanes(row_lane, eye)
    col_sub = to_sublanes(col_lane, eye)
    rank = jnp.sum(jnp.where(key_lane < key_sub, 1, 0), axis=1, keepdims=True)
    less = jnp.sum(jnp.where(row_lane < row_sub, 1, 0), axis=1, keepdims=True)
    keep = jnp.where(rank == less, 0, 1)
    packed = (key_sub - row_sub * 256) + keep * 256 + col_sub * 512
    order = jnp.sum(jnp.where(rank == lane, packed, 0), axis=0, keepdims=True)
    upto = jnp.sum(jnp.where(row_sub <= lane, 1, 0), axis=0, keepdims=True)
    count = jnp.sum(jnp.where(row_sub == lane, 1, 0), axis=0, keepdims=True)
    return order, upto - 1, count


def kernel(
    nr, nd, inner_hbm, ipat_hbm, bnd_hbm, bpat_hbm, send_hbm, rhs_hbm, init_hbm, x_hbm, r_hbm, d_hbm, w_hbm, alpha_hbm,
    ipat, bpat, send_list, q, qb, r, wb, x, rhs, w, d, alpha, v, run, runb, prodb, out_box, tab, tab_s, slots,
    local_sem, out_sem, in_sem, sems, *in_box,
):
    n_inner = q.shape[0]
    halo = out_box.shape[2]
    n_bnd = 4 * halo
    blocks = v.shape[0]
    chains = v.shape[1]
    region, dev = lax.axis_index("region"), lax.axis_index("dev")
    n_all = nr * nd
    me = region * nd + dev

    def each_peer(action):
        if n_all <= 16:
            for t in range(1, n_all):
                action(t)
        else:
            lax.fori_loop(1, n_all, lambda t, _: (action(t), 0)[1], 0)

    chunk = n_inner // 4
    loads = [pltpu.make_async_copy(init_hbm, x, local_sem.at[0])]
    for i in range(4):
        part_of = pl.ds(i * chunk, chunk)
        loads.append(pltpu.make_async_copy(inner_hbm.at[0, part_of], q.at[part_of], local_sem.at[1 + i]))
    loads.append(pltpu.make_async_copy(bnd_hbm.at[0], qb, local_sem.at[5]))
    loads.append(pltpu.make_async_copy(rhs_hbm, rhs, local_sem.at[6]))
    patterns = [
        pltpu.make_async_copy(ipat_hbm, ipat, local_sem.at[10]),
        pltpu.make_async_copy(bpat_hbm, bpat, local_sem.at[11]),
        pltpu.make_async_copy(send_hbm, send_list, local_sem.at[12]),
    ]
    for load in patterns + loads[:1]:
        load.start()

    barrier = pltpu.get_barrier_semaphore()
    def greet(t):
        peer = lax.rem(me + t, n_all)
        pl.semaphore_signal(
            barrier, inc=1, device_id={"region": peer // nd, "dev": lax.rem(peer, nd)}, device_id_type=MESH
        )

    each_peer(greet)

    targets = (
        {"dev": lax.rem(dev + nd - 1, nd)},
        {"dev": lax.rem(dev + 1, nd)},
        {"region": lax.rem(region + nr - 1, nr)},
        {"region": lax.rem(region + 1, nr)},
    )
    arrives_at = (1, 0, 3, 2)

    def cols(b):
        return pl.ds(pl.multiple_of(b * 128, 128), 128)

    def box_copy(turn, k):
        return pltpu.make_async_remote_copy(
            src_ref=out_box.at[turn, k],
            dst_ref=in_box[turn * 4 + arrives_at[k]],
            send_sem=out_sem.at[turn, k],
            recv_sem=in_sem.at[turn, arrives_at[k]],
            device_id=targets[k],
            device_id_type=MESH,
        )

    def send_halo(turn, block_of):
        for k in (0, 1, 2, 3):
            for e in range(halo):
                out_box[turn, k, e] = block_of(send_list[0, k, e]).astype(jnp.bfloat16)
            if turn == 0 and k == 0:
                pl.semaphore_wait(barrier, n_all - 1)
            box_copy(turn, k).start()

    def apply_parts(turn):
        def inner_step(s, acc):
            word = tab_s[0, s]
            entry, keep, col = word & 255, (word >> 8) & 1, word >> 9
            product = jnp.dot(v[col], q[entry], preferred_element_type=F32)
            acc = jnp.where(jnp.full((chains, 128), keep) != 0, acc, 0.0) + product
            run[s] = acc
            return acc

        lax.fori_loop(0, n_inner, inner_step, jnp.zeros((chains, 128), F32), unroll=32)
        for k in (2, 3, 0, 1):
            box_copy(turn, arrives_at[k]).wait_recv()

            def far_step(e, _):
                prodb[k * halo + e] = lax.dot_general(
                    in_box[turn * 4 + k][bpat[0, k, 1, e]],
                    qb[k, e],
                    (((1,), (1,)), ((), ())),
                    preferred_element_type=F32,
                )
                return 0

            lax.fori_loop(0, halo, far_step, 0, unroll=True)

        def gather_step(s, acc):
            word = tab_s[2, s]
            entry, keep = word & 255, (word >> 8) & 1
            acc = jnp.where(jnp.full((chains, 128), keep) != 0, acc, 0.0) + prodb[entry]
            runb[s] = acc
            return acc

        lax.fori_loop(0, n_bnd, gather_step, jnp.zeros((chains, 128), F32), unroll=8)

    def mapped_of(b):
        return run[tab_s[1, b]] + runb[tab_s[3, b]]

    chain = lax.broadcasted_iota(I32, (chains, 128), 0)
    lane = lax.broadcasted_iota(I32, (chains, 128), 1)

    def all_sum(turn, sums):
        packed = jnp.zeros((chains, 128), F32)
        for j, value in enumerate(sums):
            packed = packed + jnp.where(
                lane == chain + j * chains, jnp.sum(value, axis=1, keepdims=True), 0.0
            )
        row = jnp.sum(packed, axis=0, keepdims=True)
        slots[turn, me] = row

        def copy(t, at):
            peer = lax.rem(me + t, n_all)
            slot = me if at else peer
            return pltpu.make_async_remote_copy(
                src_ref=slots.at[turn, me],
                dst_ref=slots.at[turn, slot],
                send_sem=sems.at[turn, 0, peer],
                recv_sem=sems.at[turn, 1, slot],
                device_id={"region": peer // nd, "dev": lax.rem(peer, nd)},
                device_id_type=MESH,
            )

        each_peer(lambda t: copy(t, True).start())
        unsent.append(lambda: each_peer(lambda t: copy(t, True).wait_send()))

        def finish():
            each_peer(lambda t: copy(t, False).wait_recv())
            total = jnp.sum(slots[turn].reshape(n_all, 128), axis=0, keepdims=True)
            return [
                jnp.sum(jnp.where(lane == chain + j * chains, total, 0.0), axis=1, keepdims=True)
                for j in range(len(sums))
            ]

        return finish

    unsent = []
    zero = jnp.zeros((chains, 128), F32)

    for load in patterns + loads[:1]:
        load.wait()
    for load in loads[1:]:
        load.start()
    def round_step(b, _):
        v[b] = x[:, cols(b)].astype(jnp.bfloat16)
        return 0

    lax.fori_loop(0, blocks, round_step, 0, unroll=4)
    send_halo(0, lambda b: v[b])
    order, last, count = sort_tables(ipat[0, 1:2, :], ipat[0, 0:1, :], n_inner)
    tab[0:1, 0:n_inner] = order
    tab[1:2, 0:n_inner] = jnp.where(count > 0, last, n_inner)
    lane128 = lax.broadcasted_iota(I32, (1, 128), 1)
    brow = jnp.full((1, 128), 1 << 20, I32)
    for k in range(4):
        for e in range(halo):
            brow = jnp.where(lane128 == k * halo + e, bpat[0, k, 0, e], brow)
    order, last, count = sort_tables(brow, jnp.zeros((1, 128), I32), 128)
    tab[2:3, 0:128] = order
    tab[3:4, 0:128] = jnp.where(count > 0, last, n_bnd)
    tables = pltpu.make_async_copy(tab, tab_s, local_sem.at[7])
    tables.start()
    run[n_inner] = jnp.zeros((chains, 128), F32)
    runb[n_bnd] = jnp.zeros((chains, 128), F32)

    tables.wait()
    for load in loads[1:]:
        load.wait()
    apply_parts(0)

    def first_step(b, _):
        value = rhs[:, cols(b)] - mapped_of(b)
        r[b] = value
        v[b] = value.astype(jnp.bfloat16)
        return 0

    lax.fori_loop(0, blocks, first_step, 0, unroll=4)
    send_halo(1, lambda b: v[b])
    apply_parts(1)

    def dots_step(b, sums):
        value = mapped_of(b)
        res = r[b]
        wb[b] = value
        return sums[0] + res * res, sums[1] + res * value, sums[2] + value * value

    sums = lax.fori_loop(0, blocks, dots_step, (zero, zero, zero), unroll=4)
    norm, cross, square = all_sum(0, sums)()
    step = norm / cross
    norm_next = norm - 2.0 * step * cross + step * step * square
    ratio = norm_next / norm
    step_b = jnp.broadcast_to(step, (chains, 128))
    ratio_b = jnp.broadcast_to(ratio, (chains, 128))

    def updated(b):
        old = r[b]
        value = old - step_b * wb[b]
        return value, value + ratio_b * old

    send_halo(2, lambda b: updated(b)[1])

    def update_step(b, rr):
        value, along = updated(b)
        rhs[:, cols(b)] = value
        d[:, cols(b)] = along
        v[b] = along.astype(jnp.bfloat16)
        return rr + value * value

    rr = lax.fori_loop(0, blocks, update_step, zero, unroll=4)
    stores = [
        pltpu.make_async_copy(rhs, r_hbm, local_sem.at[9]),
        pltpu.make_async_copy(d, d_hbm, local_sem.at[10]),
    ]
    for store in stores:
        store.start()
    apply_parts(2)

    def last_dot_step(b, total):
        value = mapped_of(b)
        w[:, cols(b)] = value
        return total + d[:, cols(b)] * value

    dw = lax.fori_loop(0, blocks, last_dot_step, zero, unroll=4)
    stores.append(pltpu.make_async_copy(w, w_hbm, local_sem.at[13]))
    stores[-1].start()
    finish = all_sum(1, (rr, dw))

    def x_step(b, _):
        x[:, cols(b)] = x[:, cols(b)] + step_b * r[b]
        return 0

    lax.fori_loop(0, blocks, x_step, 0, unroll=4)
    stores.append(pltpu.make_async_copy(x, x_hbm, local_sem.at[8]))
    stores[-1].start()
    norm, curve = finish()
    step_c = jnp.broadcast_to(norm / curve, (chains, 128))

    alpha[...] = step_c
    stores.append(pltpu.make_async_copy(alpha, alpha_hbm, local_sem.at[14]))
    stores[-1].start()
    for turn in range(3):
        for k in range(4):
            box_copy(turn, k).wait_send()
    for wait in unsent:
        wait()
    for store in stores:
        store.wait()


def per_device(nr, nd, inner_blocks, inner_pattern, boundary_blocks, boundary_pattern, send_list, right_side, initial):
    n_inner, blk = inner_blocks.shape[1], inner_blocks.shape[2]
    halo = send_list.shape[2]
    chains, nodes = right_side.shape
    blocks = nodes // blk
    anywhere = pl.BlockSpec(memory_space=pl.ANY)
    vector = pltpu.VMEM((chains, nodes), F32)
    x, r, d, w, step = pl.pallas_call(
        functools.partial(kernel, nr, nd),
        out_shape=(jax.ShapeDtypeStruct((chains, nodes), F32),) * 4
        + (jax.ShapeDtypeStruct((chains, 128), F32),),
        in_specs=[pl.BlockSpec(memory_space=pltpu.HBM)] * 7,
        out_specs=(anywhere,) * 5,
        scratch_shapes=[
            pltpu.VMEM(inner_pattern.shape, I32),
            pltpu.SMEM(boundary_pattern.shape, I32),
            pltpu.SMEM(send_list.shape, I32),
            pltpu.VMEM((n_inner, blk, blk), jnp.bfloat16),
            pltpu.VMEM((4, halo, blk, blk), jnp.bfloat16),
            pltpu.VMEM((blocks, chains, blk), F32),
            pltpu.VMEM((blocks, chains, blk), F32),
            vector,
            vector,
            vector,
            vector,
            pltpu.VMEM((chains, 128), F32),
            pltpu.VMEM((blocks, chains, blk), jnp.bfloat16),
            pltpu.VMEM((n_inner + 1, chains, blk), F32),
            pltpu.VMEM((4 * halo + 1, chains, blk), F32),
            pltpu.VMEM((4 * halo, chains, blk), F32),
            pltpu.VMEM((3, 4, halo, chains, blk), jnp.bfloat16),
            pltpu.VMEM((8, 256), I32),
            pltpu.SMEM((8, 256), I32),
            pltpu.VMEM((ITERS, nr * nd, 1, 128), F32),
            pltpu.SemaphoreType.DMA((15,)),
            pltpu.SemaphoreType.DMA((3, 4)),
            pltpu.SemaphoreType.DMA((3, 4)),
            pltpu.SemaphoreType.DMA((ITERS, 2, nr * nd)),
        ]
        + [pltpu.VMEM((halo, chains, blk), jnp.bfloat16)] * 12,
        compiler_params=pltpu.CompilerParams(
            collective_id=0, has_side_effects=True, vmem_limit_bytes=48 * 1024 * 1024
        ),
    )(inner_blocks, inner_pattern, boundary_blocks, boundary_pattern, send_list, right_side, initial)
    step = step[:, :1]
    return x + step * d, r - step * w


def solution(mesh):
    spread = ("groups", "region", "dev")
    return jax.shard_map(
        functools.partial(per_device, mesh.shape["region"], mesh.shape["dev"]),
        mesh=mesh,
        in_specs=(
            P(spread, None, None, None),
            P(spread, None, None),
            P(spread, None, None, None, None),
            P(spread, None, None, None),
            P(spread, None, None),
            P(None, spread),
            P(None, spread),
        ),
        out_specs=(P(None, spread), P(None, spread)),
        check_vma=False,
    )
```

time: 48 us -> 42.2 us (0.88)
  local copies, waits for them, and re-layouts: 7.84 us -> 3.38 us
  Pallas kernels: 39.2 us -> 36.3 us
  other arithmetic: 0 us -> 1.6 us
    unnamed x14 -> x8, local copies, waits for them, and re-layouts: 7.84 us -> 3.27 us
    pallas_call x1, Pallas kernels: 39.2 us -> 36.3 us  [per_device(): pl.pallas_call(functools.partial(kernel, nr, nd), out_shape=(jax.ShapeDty...]
    sub x0 -> x1, other arithmetic: none -> 1.6 us  [per_device(): return (x + step * d, r - step * w)]
where the time goes in v2:
time: 42.2 us; the launch traced here: 41.9 us
  Pallas kernels  36.3 us (86%)
  local copies, waits for them, and re-layouts  3.38 us (8%)
  other arithmetic  1.6 us (4%)
  between operations  0.65 us (2%)
    pallas_call x1, Pallas kernels, per_device(): pl.pallas_call(functools.partial(kernel, nr, nd), out_shape=(jax.ShapeDty...  36.3 us
    unnamed x8, local copies, waits for them, and re-layouts  3.27 us
    sub x1, other arithmetic, per_device(): return (x + step * d, r - step * w)  1.6 us

profile of v2, /device:TPU:0, one launch (start us, length us, event | category | flops | bytes accessed | tf_op | source)
XLA Modules:
  0.0 41.9 jit_solution(8799607964227845112)
XLA Ops:
  0.6 0.0 copy-start
  0.6 1.2 %copy-done = f32[32,8192]{1,0:T(8,128)S(1)} copy-done((f32[32,8192]{1,0:T(8,128)S(1)}, f32[32,8192]{1,0:T(8,128)}, u32[]{:S(2)}) %copy-start) | copy-done | bytes 1048600
  1.9 0.0 copy-start.1
  1.9 0.7 %copy-done.1 = s32[1,4,2,12]{3,2,1,0:T(2,128)S(1)} copy-done((s32[1,4,2,12]{3,2,1,0:T(2,128)S(1)}, s32[1,4,2,12]{3,2,1,0:T(2,128)}, u32[]{:S(2)}) %copy-start.1) | copy-done | bytes 408
  2.5 0.0 copy-start.2
  2.5 0.7 %copy-done.2 = s32[1,2,192]{2,1,0:T(2,128)S(1)} copy-done((s32[1,2,192]{2,1,0:T(2,128)S(1)}, s32[1,2,192]{2,1,0:T(2,128)}, u32[]{:S(2)}) %copy-start.2) | copy-done | bytes 1560
  3.2 0.0 copy-start.3
  3.2 0.7 %copy-done.3 = s32[1,4,12]{2,1,0:T(4,128)S(1)} copy-done((s32[1,4,12]{2,1,0:T(4,128)S(1)}, s32[1,4,12]{2,1,0:T(4,128)}, u32[]{:S(2)}) %copy-start.3) | copy-done | bytes 216
  3.9 36.3 %shard_map.86 = (f32[32,8192]{1,0:T(8,128)S(1)}, f32[32,8192]{1,0:T(8,128)S(1)}, f32[32,8192]{1,0:T(8,128)S(1)}, f32[32,8192]{1,0:T(8,128)S(1)}, f32[32,128]{1,0:T(8,128)S(1)}) custom-call(bf16[1,192,128,128]{3,2,1,0:T(8,128)(2,1)} %inner_hbm.1, s32[1,2,192]{2,1,0:T(2,128)S(1)} %copy-done.2, bf16[1,4,12,128,128]{4,3,2,1,0:T(8,128)(2,1)} %bnd_hbm.1, ...), custom_call_target="tpu_custom_call" | custom-call | tf_op jit(solution)/shard_map/pallas_call | solution.py:305
  40.2 0.1 slice_reduce_fusion
  40.3 1.6 %multiply_subtract_fusion = (f32[32,8192]{1,0:T(8,128)}, f32[32,8192]{1,0:T(8,128)}) fusion(f32[32,8192]{1,0:T(8,128)S(1)} %get-tuple-element.10, f32[32,8192]{1,0:T(8,128)S(1)} %get-tuple-element.11, f32[32]{0:T(128)S(1)} %slice_reduce_fusion, f32[32,8192]{1,0:T(8,128)S(1)} %get-tuple-element.7, f32[32,8192]{1,0:T(8,128)S(1)} %get-tuple-element.9), kind=kLoop, calls=%fused_computation | loop fusion | flops 1048576 | bytes 6291584 | tf_op jit(solution)/shard_map/sub | solution.py:343
Async XLA Ops:
  0.6 1.2 %copy-start = (f32[32,8192]{1,0:T(8,128)S(1)}, f32[32,8192]{1,0:T(8,128)}, u32[]{:S(2)}) copy-start(f32[32,8192]{1,0:T(8,128)} %rhs_hbm.1) | copy-start | bytes 3145732
  1.9 0.7 %copy-start.1 = (s32[1,4,2,12]{3,2,1,0:T(2,128)S(1)}, s32[1,4,2,12]{3,2,1,0:T(2,128)}, u32[]{:S(2)}) copy-start(s32[1,4,2,12]{3,2,1,0:T(2,128)} %bpat_hbm.1) | copy-start | bytes 1156
  2.5 0.7 %copy-start.2 = (s32[1,2,192]{2,1,0:T(2,128)S(1)}, s32[1,2,192]{2,1,0:T(2,128)}, u32[]{:S(2)}) copy-start(s32[1,2,192]{2,1,0:T(2,128)} %ipat_hbm.1) | copy-start | bytes 4612
  3.2 0.7 %copy-start.3 = (s32[1,4,12]{2,1,0:T(4,128)S(1)}, s32[1,4,12]{2,1,0:T(4,128)}, u32[]{:S(2)}) copy-start(s32[1,4,12]{2,1,0:T(4,128)} %send_hbm.1) | copy-start | bytes 580

commit v3 on v2

--- a/solution.py
+++ b/solution.py
@@ -158,7 +158,7 @@
         slots[turn, me] = row
 
         def copy(t, at):
-            peer = lax.rem(me + t, n_all)
+            peer = lax.rem(me + n_all - t, n_all)
             slot = me if at else peer
             return pltpu.make_async_remote_copy(
                 src_ref=slots.at[turn, me],
@@ -193,7 +193,7 @@
         v[b] = x[:, cols(b)].astype(jnp.bfloat16)
         return 0
 
-    lax.fori_loop(0, blocks, round_step, 0, unroll=4)
+    lax.fori_loop(0, blocks, round_step, 0, unroll=8)
     send_halo(0, lambda b: v[b])
     order, last, count = sort_tables(ipat[0, 1:2, :], ipat[0, 0:1, :], n_inner)
     tab[0:1, 0:n_inner] = order
@@ -222,7 +222,7 @@
         v[b] = value.astype(jnp.bfloat16)
         return 0
 
-    lax.fori_loop(0, blocks, first_step, 0, unroll=4)
+    lax.fori_loop(0, blocks, first_step, 0, unroll=8)
     send_halo(1, lambda b: v[b])
     apply_parts(1)
 
@@ -232,7 +232,7 @@
         wb[b] = value
         return sums[0] + res * res, sums[1] + res * value, sums[2] + value * value
 
-    sums = lax.fori_loop(0, blocks, dots_step, (zero, zero, zero), unroll=4)
+    sums = lax.fori_loop(0, blocks, dots_step, (zero, zero, zero), unroll=8)
     norm, cross, square = all_sum(0, sums)()
     step = norm / cross
     norm_next = norm - 2.0 * step * cross + step * step * square
@@ -254,7 +254,7 @@
         v[b] = along.astype(jnp.bfloat16)
         return rr + value * value
 
-    rr = lax.fori_loop(0, blocks, update_step, zero, unroll=4)
+    rr = lax.fori_loop(0, blocks, update_step, zero, unroll=8)
     stores = [
         pltpu.make_async_copy(rhs, r_hbm, local_sem.at[9]),
         pltpu.make_async_copy(d, d_hbm, local_sem.at[10]),
@@ -268,7 +268,7 @@
         w[:, cols(b)] = value
         return total + d[:, cols(b)] * value
 
-    dw = lax.fori_loop(0, blocks, last_dot_step, zero, unroll=4)
+    dw = lax.fori_loop(0, blocks, last_dot_step, zero, unroll=8)
     stores.append(pltpu.make_async_copy(w, w_hbm, local_sem.at[13]))
     stores[-1].start()
     finish = all_sum(1, (rr, dw))
@@ -277,7 +277,7 @@
         x[:, cols(b)] = x[:, cols(b)] + step_b * r[b]
         return 0
 
-    lax.fori_loop(0, blocks, x_step, 0, unroll=4)
+    lax.fori_loop(0, blocks, x_step, 0, unroll=8)
     stores.append(pltpu.make_async_copy(x, x_hbm, local_sem.at[8]))
     stores[-1].start()
     norm, curve = finish()
@@ -336,7 +336,7 @@
         ]
         + [pltpu.VMEM((halo, chains, blk), jnp.bfloat16)] * 12,
         compiler_params=pltpu.CompilerParams(
-            collective_id=0, has_side_effects=True, vmem_limit_bytes=48 * 1024 * 1024
+            collective_id=0, has_side_effects=True, vmem_limit_bytes=49 * 1024 * 1024
         ),
     )(inner_blocks, inner_pattern, boundary_blocks, boundary_pattern, send_list, right_side, initial)
     step = step[:, :1]

time: 42.2 us -> 40.9 us (0.969)
  local copies, waits for them, and re-layouts: 3.38 us -> 2.15 us
    unnamed x8 -> x6, local copies, waits for them, and re-layouts: 3.27 us -> 2.04 us
where the time goes in v3:
time: 40.9 us; the launch traced here: 40.6 us
  Pallas kernels  36.2 us (89%)
  local copies, waits for them, and re-layouts  2.15 us (5%)
  other arithmetic  1.6 us (4%)
  between operations  0.65 us (2%)
    pallas_call x1, Pallas kernels, per_device(): pl.pallas_call(functools.partial(kernel, nr, nd), out_shape=(jax.ShapeDty...  36.2 us
    unnamed x6, local copies, waits for them, and re-layouts  2.04 us
    sub x1, other arithmetic, per_device(): return (x + step * d, r - step * w)  1.6 us

profile of v3, /device:TPU:0, one launch (start us, length us, event | category | flops | bytes accessed | tf_op | source)
XLA Modules:
  0.0 40.6 jit_solution(8435005648588941548)
XLA Ops:
  0.6 0.0 copy-start
  0.6 0.7 %copy-done = s32[1,4,2,12]{3,2,1,0:T(2,128)S(1)} copy-done((s32[1,4,2,12]{3,2,1,0:T(2,128)S(1)}, s32[1,4,2,12]{3,2,1,0:T(2,128)}, u32[]{:S(2)}) %copy-start) | copy-done | bytes 408
  1.3 0.0 copy-start.1
  1.3 0.7 %copy-done.1 = s32[1,2,192]{2,1,0:T(2,128)S(1)} copy-done((s32[1,2,192]{2,1,0:T(2,128)S(1)}, s32[1,2,192]{2,1,0:T(2,128)}, u32[]{:S(2)}) %copy-start.1) | copy-done | bytes 1560
  2.0 0.0 copy-start.2
  2.0 0.7 %copy-done.2 = s32[1,4,12]{2,1,0:T(4,128)S(1)} copy-done((s32[1,4,12]{2,1,0:T(4,128)S(1)}, s32[1,4,12]{2,1,0:T(4,128)}, u32[]{:S(2)}) %copy-start.2) | copy-done | bytes 216
  2.7 36.2 %shard_map.86 = (f32[32,8192]{1,0:T(8,128)S(1)}, f32[32,8192]{1,0:T(8,128)S(1)}, f32[32,8192]{1,0:T(8,128)S(1)}, f32[32,8192]{1,0:T(8,128)S(1)}, f32[32,128]{1,0:T(8,128)S(1)}) custom-call(bf16[1,192,128,128]{3,2,1,0:T(8,128)(2,1)} %inner_hbm.1, s32[1,2,192]{2,1,0:T(2,128)S(1)} %copy-done.1, bf16[1,4,12,128,128]{4,3,2,1,0:T(8,128)(2,1)} %bnd_hbm.1, ...), custom_call_target="tpu_custom_call" | custom-call | tf_op jit(solution)/shard_map/pallas_call | solution.py:305
  38.9 0.1 slice_reduce_fusion
  39.0 1.6 %multiply_subtract_fusion = (f32[32,8192]{1,0:T(8,128)}, f32[32,8192]{1,0:T(8,128)}) fusion(f32[32,8192]{1,0:T(8,128)S(1)} %get-tuple-element.10, f32[32,8192]{1,0:T(8,128)S(1)} %get-tuple-element.11, f32[32]{0:T(128)S(1)} %slice_reduce_fusion, f32[32,8192]{1,0:T(8,128)S(1)} %get-tuple-element.7, f32[32,8192]{1,0:T(8,128)S(1)} %get-tuple-element.9), kind=kLoop, calls=%fused_computation | loop fusion | flops 1048576 | bytes 6291584 | tf_op jit(solution)/shard_map/sub | solution.py:343
Async XLA Ops:
  0.6 0.7 %copy-start = (s32[1,4,2,12]{3,2,1,0:T(2,128)S(1)}, s32[1,4,2,12]{3,2,1,0:T(2,128)}, u32[]{:S(2)}) copy-start(s32[1,4,2,12]{3,2,1,0:T(2,128)} %bpat_hbm.1) | copy-start | bytes 1156
  1.3 0.7 %copy-start.1 = (s32[1,2,192]{2,1,0:T(2,128)S(1)}, s32[1,2,192]{2,1,0:T(2,128)}, u32[]{:S(2)}) copy-start(s32[1,2,192]{2,1,0:T(2,128)} %ipat_hbm.1) | copy-start | bytes 4612
  2.0 0.7 %copy-start.2 = (s32[1,4,12]{2,1,0:T(4,128)S(1)}, s32[1,4,12]{2,1,0:T(4,128)}, u32[]{:S(2)}) copy-start(s32[1,4,12]{2,1,0:T(4,128)} %send_hbm.1) | copy-start | bytes 580
